TPU v7x, 32 devices: a whole 2x2x4 slice. The times are simulated.
32 devices in a mesh: row: 8 (over y, x, core), col: 4 (over z).
Axes of the slice: x: 2, y: 2, z: 4, core: 2. Of those that a mesh axis runs over, the one named last changes fastest.
Arguments:
- blocks: float32 [8, 4, 288, 4096], P('row', 'col')
- block_slot: int32 [8, 4, 288], P('row', 'col'), may hold values from 0 to 73727, as said below
- sign_vec: int32 [98304], P(('col', 'row')), may hold values from -1 to 1, as said below
Outputs:
- normed_image: float32 [98304, 64], P(('col', 'row'))
- power_image: float32 [98304, 64], P(('col', 'row'))
Inputs may be any that keep to these rules, and one draw needn't show every extreme that they name: `block_slot`: each entry is i * 192 + j for a local block row i and block column j; the entries of one device are distinct, and each device names slot 0 and the last slot. `sign_vec`: every entry is -1 or 1.
All inputs are finite; a program needn't handle non-finite values.
Results may differ from a plain program's by a relative error of at most 0.0001.
Values sent between devices are 32-bit elements; how exact they have to be, the bound alone decides.
A program may use at most 128 MiB of HBM per device.

v0:
```python
import jax
import jax.numpy as jnp
from jax import lax
from jax.sharding import PartitionSpec as P

BLOCK = 64
PROBES = 64


def hadamard_sign(row_ids, probe_count):
    low_bits = row_ids % 128
    probe_ids = jnp.arange(probe_count, dtype=jnp.int32)
    parity = jnp.zeros((row_ids.shape[0], probe_count), jnp.int32)
    for bit_pos in range(7):
        left_bit = jnp.bitwise_and(jnp.right_shift(low_bits, bit_pos), 1)
        right_bit = jnp.bitwise_and(jnp.right_shift(probe_ids, bit_pos), 1)
        parity = parity + left_bit[:, None] * right_bit[None, :]
    return (1 - 2 * (parity % 2)).astype(jnp.float32)


def block_products(tiles, field, sources, targets, target_count, transpose):
    probe_count = field.shape[1]
    picked = field.reshape(-1, BLOCK, probe_count)[sources]
    pattern_text = "bji,bjk->bik" if transpose else "bij,bjk->bik"
    products = jnp.einsum(pattern_text, tiles, picked, precision=lax.Precision.HIGHEST)
    one_hot = (targets[None, :] == jnp.arange(target_count, dtype=jnp.int32)[:, None]).astype(
        jnp.float32
    )
    summed = jnp.dot(
        one_hot,
        products.reshape(tiles.shape[0], BLOCK * probe_count),
        precision=lax.Precision.HIGHEST,
        preferred_element_type=jnp.float32,
    )
    return summed.reshape(target_count * BLOCK, probe_count)


def local(blocks, block_slot, sign_vec):
    local_rows = sign_vec.shape[0]
    n_rows_axis = lax.axis_size("row")
    n_cols_axis = lax.axis_size("col")
    total_rows = local_rows * n_rows_axis * n_cols_axis
    band_rows = total_rows // n_cols_axis
    row_blocks = band_rows // BLOCK
    col_blocks = total_rows // n_rows_axis // BLOCK
    row_index = lax.axis_index("row")
    col_index = lax.axis_index("col")
    tiles = blocks.reshape(-1, BLOCK, BLOCK)
    slots = block_slot.reshape(-1)
    blk_row = slots // col_blocks
    blk_col = slots % col_blocks
    own_ids = (
        col_index * band_rows + row_index * local_rows + jnp.arange(local_rows, dtype=jnp.int32)
    )
    own_panel = sign_vec.astype(jnp.float32)[:, None] * hadamard_sign(own_ids, PROBES)
    panel = lax.all_gather(own_panel, "col", axis=0, tiled=True)
    partial_value = block_products(tiles, panel, blk_col, blk_row, row_blocks, False)
    first_own = lax.psum_scatter(partial_value, "row", scatter_dimension=0, tiled=True)
    col_sums = lax.psum(jnp.sum(first_own * first_own, axis=0), ("row", "col"))
    normed_own = first_own / jnp.sqrt(col_sums / total_rows + 1e-06)
    normed_col_band = lax.all_gather(normed_own, "row", axis=0, tiled=True)
    second_partial = block_products(tiles, normed_col_band, blk_row, blk_col, col_blocks, True)
    power_own = lax.psum_scatter(second_partial, "col", scatter_dimension=0, tiled=True)
    return (normed_own, power_own)


def solution(mesh):
    in_specs = (P("row", "col", None, None), P("row", "col", None), P(("col", "row")))
    out_specs = (P(("col", "row"), None), P(("col", "row"), None))
    return jax.shard_map(local, mesh=mesh, in_specs=in_specs, out_specs=out_specs, check_vma=False)
```

profile of v0, /device:TPU:0, one launch (start us, length us, event | category | flops | bytes accessed | tf_op | source)
XLA Modules:
  0.0 573.4 jit_solution(14866779846421602721)
XLA Ops:
  7.2 0.0 all-gather.3.cloned.1.call-start
  7.3 0.7 convert_element_type.8
  8.1 4.6 fusion.4
  12.7 0.0 all-gather.3.cloned.1.call-update
  12.7 0.0 reduce-scatter.3.cloned.1.call-start
  12.7 6.2 %copy.7 = f32[1,1,288,4096]{2,3,1,0:T(8,128)} copy(f32[1,1,288,4096]{3,2,1,0:T(8,128)} %param.3) | data formatting | bytes 9437184 | tf_op args[0]
  19.0 0.0 copy-start.2
  19.0 12.3 %copy.9 = f32[288,64,64]{2,1,0:T(8,128)} copy(f32[288,64,64]{0,2,1:T(8,128)} %bitcast.32) | data formatting | bytes 9437184 | tf_op jit(solution)/shard_map/reshape | solution.py:48
  31.2 0.0 copy-done.2
  31.4 99.5 %all-gather.3.cloned.1.call-done = f32[12288,64]{1,0:T(8,128)} async-done(((f32[3072,64]{1,0:T(8,128)}), f32[12288,64]{1,0:T(8,128)}) %all-gather.3.cloned.1.call-update) | async-done | bytes 3145744 | tf_op jit(solution)/shard_map/all_gather | solution.py:56
  130.9 7.6 %gather_fusion = f32[288,64,64]{2,1,0:T(8,128)} fusion(f32[192,64,64]{2,1,0:T(8,128)} %bitcast.33, s32[1024]{0:T(1024)S(1)} %pad_clamp_fusion.1), kind=kCustom, calls=%fused_computation | custom fusion | bytes 9438336 | tf_op jit(solution)/shard_map/gather | solution.py:23
  138.5 21.5 %convolution_bitcast_fusion.1 = f32[288,64,64]{1,2,0:T(8,128)} fusion(f32[288,64,64]{2,1,0:T(8,128)} %gather_fusion, f32[288,64,64]{2,1,0:T(8,128)} %copy.9), kind=kOutput, calls=%fused_computation.3 | convolution fusion | flops 905969664 | bytes 14155776 | tf_op jit(solution)/shard_map/bij,bjk->bik/dot_general | solution.py:25
  159.9 11.7 %copy.10 = f32[288,64,64]{0,2,1:T(8,128)} copy(f32[288,64,64]{1,2,0:T(8,128)} %convolution_bitcast_fusion.1) | data formatting | bytes 9437184 | tf_op jit(solution)/shard_map/bij,bjk->bik/dot_general | solution.py:25
  171.6 12.3 %fusion.5 = f32[384,4096]{1,0:T(8,128)} fusion(f32[288,4096]{0,1:T(8,128)} %bitcast.31, s32[288]{0:T(512)S(1)} %get-tuple-element.9), kind=kOutput, calls=%fused_computation.15 | convolution fusion | flops 5435928576 | bytes 11011200 | tf_op jit(solution)/shard_map/dot_general | solution.py:29
  183.9 10.8 %reshape.223 = f32[24576,64]{1,0:T(8,128)} reshape(f32[384,4096]{1,0:T(8,128)} %fusion.5) | data formatting | bytes 12582912 | tf_op jit(solution)/shard_map/reshape | solution.py:35
  194.7 0.0 reduce-scatter.3.cloned.1.call-update
  194.7 0.0 all-gather.5.cloned.1.call-start
  194.8 90.7 %reduce-scatter.3.cloned.1.call-done = f32[3072,64]{1,0:T(8,128)} async-done(((f32[24576,64]{1,0:T(8,128)}), f32[3072,64]{1,0:T(8,128)}) %reduce-scatter.3.cloned.1.call-update) | async-done | bytes 786448 | tf_op jit(solution)/shard_map/reduce_scatter | solution.py:58
  285.5 0.0 copy-start.1
  285.5 1.9 multiply_reduce_fusion
  287.4 39.3 %psum.7 = f32[64]{0:T(128)S(1)} all-reduce(f32[64]{0:T(128)S(1)} %multiply_reduce_fusion), channel_id=1, replica_groups=mesh['row'=8,'col'=4] {'row','col'}, use_global_device_ids=true, to_apply=%region_2.3 | all-reduce | flops 64 | bytes 512 | tf_op jit(solution)/shard_map/psum | solution.py:59
  326.8 0.0 copy-done.1
  326.8 1.3 broadcast_divide_fusion
  328.1 0.0 all-gather.5.cloned.1.call-update
  328.1 0.0 reduce-scatter.5.cloned.1.call-start
  328.2 72.7 %all-gather.5.cloned.1.call-done = f32[24576,64]{1,0:T(8,128)} async-done(((f32[3072,64]{1,0:T(8,128)}), f32[24576,64]{1,0:T(8,128)}) %all-gather.5.cloned.1.call-update) | async-done | bytes 6291472 | tf_op jit(solution)/shard_map/all_gather | solution.py:61
  400.9 9.4 %gather_fusion.1 = f32[288,64,64]{2,1,0:T(8,128)} fusion(f32[384,64,64]{2,1,0:T(8,128)} %bitcast.34, s32[1024]{0:T(1024)S(1)} %pad_clamp_fusion), kind=kCustom, calls=%fused_computation.1 | custom fusion | bytes 9438336 | tf_op jit(solution)/shard_map/gather | solution.py:23
  410.3 21.1 %convolution_bitcast_fusion = f32[288,64,64]{1,2,0:T(8,128)} fusion(f32[288,64,64]{2,1,0:T(8,128)} %gather_fusion.1, f32[288,64,64]{2,1,0:T(8,128)} %copy.9), kind=kOutput, calls=%fused_computation.2 | convolution fusion | flops 905969664 | bytes 14155776 | tf_op jit(solution)/shard_map/bji,bjk->bik/dot_general | solution.py:25
  431.4 11.6 %copy.15 = f32[288,64,64]{0,2,1:T(8,128)} copy(f32[288,64,64]{1,2,0:T(8,128)} %convolution_bitcast_fusion) | data formatting | bytes 9437184 | tf_op jit(solution)/shard_map/bji,bjk->bik/dot_general | solution.py:25
  443.0 5.9 %fusion.7 = f32[192,4096]{1,0:T(8,128)S(1)} fusion(f32[288,4096]{0,1:T(8,128)} %bitcast.30, s32[288]{0:T(512)S(1)} %get-tuple-element.8), kind=kOutput, calls=%fused_computation.18 | convolution fusion | flops 2717964288 | bytes 7865472 | tf_op jit(solution)/shard_map/dot_general | solution.py:29
  448.9 4.2 reshape.226
  453.2 0.0 copy-start
  453.2 0.0 reduce-scatter.5.cloned.1.call-update
  453.2 1.4 copy-done
  454.6 1.3 copy.16
  455.9 108.2 %reduce-scatter.5.cloned.1.call-done = f32[3072,64]{1,0:T(8,128)} async-done(((f32[12288,64]{1,0:T(8,128)}), f32[3072,64]{1,0:T(8,128)}) %reduce-scatter.5.cloned.1.call-update) | async-done | bytes 786448 | tf_op jit(solution)/shard_map/reduce_scatter | solution.py:63
  564.1 2.7 copy.17
  (15 shorter events, 0.2 us)
Async XLA Ops:
  7.2 123.7 %all-gather.3.cloned.1.call-start = ((), (), s32[]{:S(2)}) async-start(), calls=%async_computation.2 | async-start | bytes 7864320 | tf_op jit(solution)/shard_map/all_gather | solution.py:56
  12.7 272.8 %reduce-scatter.3.cloned.1.call-start = ((), (), s32[]{:S(2)}) async-start(), calls=%async_computation.3 | async-start | bytes 14155776 | tf_op jit(solution)/shard_map/reduce_scatter | solution.py:58
  19.0 12.3 %copy-start.2 = (s32[1,1,288]{2,1,0:T(1,128)S(1)}, s32[1,1,288]{2,1,0:T(1,128)}, u32[]{:S(2)}) copy-start(s32[1,1,288]{2,1,0:T(1,128)} %param.4) | copy-start | bytes 3460
  194.7 206.2 %all-gather.5.cloned.1.call-start = ((), (), s32[]{:S(2)}) async-start(), calls=%async_computation.4 | async-start | bytes 14155776 | tf_op jit(solution)/shard_map/all_gather | solution.py:61
  285.5 41.3 %copy-start.1 = (f32[3072,64]{1,0:T(8,128)S(1)}, f32[3072,64]{1,0:T(8,128)}, u32[]{:S(2)}) copy-start(f32[3072,64]{1,0:T(8,128)} %reduce-scatter.3.cloned.1.call-done) | copy-start | bytes 2359300
  328.1 236.0 %reduce-scatter.5.cloned.1.call-start = ((), (), s32[]{:S(2)}) async-start(), calls=%async_computation.5 | async-start | bytes 7864320 | tf_op jit(solution)/shard_map/reduce_scatter | solution.py:63
  453.2 1.4 copy-start
Sparse Core Ops, SparseCore 0:
  12.8 118.0 all-gather.2
  194.8 90.6 reduce-scatter.2
  328.2 72.6 all-gather.4
  453.3 110.7 reduce-scatter.4
where the time goes:
time: 574 us; the launch traced here: 573 us
  waiting for transfers between devices  371 us (65%)
  local copies, waits for them, and re-layouts  79.3 us (14%)
  matrix products  60.8 us (11%)
  blocking collectives  39.3 us (7%)
  between operations  13.9 us (2%)
  other arithmetic  8.73 us (2%)
    reduce_scatter x1, waiting for transfers between devices, local(): lax.psum_scatter(second_partial, 'col', scatter_dimension=0, tiled=True)  108 us
    all_gather x1, waiting for transfers between devices, local(): panel = lax.all_gather(own_panel, 'col', axis=0, tiled=True)  99.5 us
    reduce_scatter x1, waiting for transfers between devices, local(): lax.psum_scatter(partial_value, 'row', scatter_dimension=0, tiled=True)  90.7 us
    all_gather x1, waiting for transfers between devices, local(): normed_col_band = lax.all_gather(normed_own, 'row', axis=0, tiled=True)  72.7 us
    dot_general x2, matrix products, block_products(): jnp.einsum(pattern_text, tiles, picked, precision=lax.Precision.HIGHEST)  42.6 us
    psum x1, blocking collectives, local(): col_sums = lax.psum(jnp.sum(first_own * first_own, axis=0), ('row', 'col'))  39.3 us
    dot_general x2, local copies, waits for them, and re-layouts, block_products(): jnp.einsum(pattern_text, tiles, picked, precision=lax.Precision.HIGHEST)  23.2 us
    dot_general x2, matrix products, block_products(): jnp.dot(one_hot, products.reshape(tiles.shape[0], BLOCK * probe_count), p...  18.2 us
  transfers between devices with their start and end apart: 4, of which 4 were waited for; matrix products, arithmetic and copies ran while one was open for 3% of the time, Pallas kernels for 0%

commit v1 on v0

--- a/solution.py
+++ b/solution.py
@@ -56,7 +56,7 @@
     panel = lax.all_gather(own_panel, "col", axis=0, tiled=True)
     partial_value = block_products(tiles, panel, blk_col, blk_row, row_blocks, False)
     first_own = lax.psum_scatter(partial_value, "row", scatter_dimension=0, tiled=True)
-    col_sums = lax.psum(jnp.sum(first_own * first_own, axis=0), ("row", "col"))
+    col_sums = lax.psum(lax.psum(jnp.sum(first_own * first_own, axis=0), "col"), "row")
     normed_own = first_own / jnp.sqrt(col_sums / total_rows + 1e-06)
     normed_col_band = lax.all_gather(normed_own, "row", axis=0, tiled=True)
     second_partial = block_products(tiles, normed_col_band, blk_row, blk_col, col_blocks, True)

time: 574 us -> 555 us (0.967)
  blocking collectives: 39.3 us -> 23.5 us
    psum x1 -> x2, blocking collectives: 39.3 us -> 23.5 us  [the longest x1 11.8 us: local(): lax.psum(lax.psum(jnp.sum(first_own * first_own, axis=0), 'col'), 'row')]
  transfers between devices with their start and end apart: 4 -> 4, of which waited for: 4 -> 4; matrix products, arithmetic and copies ran while one was open for 3% -> 4% of each run, Pallas kernels for 0% -> 0%
where the time goes in v1:
time: 555 us; the launch traced here: 554 us
  waiting for transfers between devices  368 us (66%)
  local copies, waits for them, and re-layouts  79.3 us (14%)
  matrix products  60.8 us (11%)
  blocking collectives  23.5 us (4%)
  between operations  13.9 us (3%)
  other arithmetic  8.74 us (2%)
    reduce_scatter x1, waiting for transfers between devices, local(): lax.psum_scatter(second_partial, 'col', scatter_dimension=0, tiled=True)  108 us
    all_gather x1, waiting for transfers between devices, local(): panel = lax.all_gather(own_panel, 'col', axis=0, tiled=True)  99.5 us
    reduce_scatter x1, waiting for transfers between devices, local(): lax.psum_scatter(partial_value, 'row', scatter_dimension=0, tiled=True)  90.7 us
    all_gather x1, waiting for transfers between devices, local(): normed_col_band = lax.all_gather(normed_own, 'row', axis=0, tiled=True)  69.3 us
    dot_general x2, matrix products, block_products(): jnp.einsum(pattern_text, tiles, picked, precision=lax.Precision.HIGHEST)  42.6 us
    dot_general x2, local copies, waits for them, and re-layouts, block_products(): jnp.einsum(pattern_text, tiles, picked, precision=lax.Precision.HIGHEST)  23.2 us
    dot_general x2, matrix products, block_products(): jnp.dot(one_hot, products.reshape(tiles.shape[0], BLOCK * probe_count), p...  18.2 us
    gather x2, local copies, waits for them, and re-layouts, block_products(): picked = field.reshape(-1, BLOCK, probe_count)[sources]  17 us
  transfers between devices with their start and end apart: 4, of which 4 were waited for; matrix products, arithmetic and copies ran while one was open for 4% of the time, Pallas kernels for 0%

profile of v1, /device:TPU:0, one launch (start us, length us, event | category | flops | bytes accessed | tf_op | source)
XLA Modules:
  0.0 554.1 jit_solution(6257303504813455373)
XLA Ops:
  7.2 0.0 all-gather.3.cloned.1.call-start
  7.3 0.7 convert_element_type.8
  8.1 4.6 fusion.4
  12.7 0.0 all-gather.3.cloned.1.call-update
  12.7 0.0 reduce-scatter.3.cloned.1.call-start
  12.7 6.2 %copy.7 = f32[1,1,288,4096]{2,3,1,0:T(8,128)} copy(f32[1,1,288,4096]{3,2,1,0:T(8,128)} %param.3) | data formatting | bytes 9437184 | tf_op args[0]
  19.0 0.0 copy-start.2
  19.0 12.3 %copy.9 = f32[288,64,64]{2,1,0:T(8,128)} copy(f32[288,64,64]{0,2,1:T(8,128)} %bitcast.32) | data formatting | bytes 9437184 | tf_op jit(solution)/shard_map/reshape | solution.py:48
  31.2 0.0 copy-done.2
  31.4 99.5 %all-gather.3.cloned.1.call-done = f32[12288,64]{1,0:T(8,128)} async-done(((f32[3072,64]{1,0:T(8,128)}), f32[12288,64]{1,0:T(8,128)}) %all-gather.3.cloned.1.call-update) | async-done | bytes 3145744 | tf_op jit(solution)/shard_map/all_gather | solution.py:56
  130.9 7.6 %gather_fusion = f32[288,64,64]{2,1,0:T(8,128)} fusion(f32[192,64,64]{2,1,0:T(8,128)} %bitcast.33, s32[1024]{0:T(1024)S(1)} %pad_clamp_fusion.1), kind=kCustom, calls=%fused_computation | custom fusion | bytes 9438336 | tf_op jit(solution)/shard_map/gather | solution.py:23
  138.5 21.5 %convolution_bitcast_fusion.1 = f32[288,64,64]{1,2,0:T(8,128)} fusion(f32[288,64,64]{2,1,0:T(8,128)} %gather_fusion, f32[288,64,64]{2,1,0:T(8,128)} %copy.9), kind=kOutput, calls=%fused_computation.3 | convolution fusion | flops 905969664 | bytes 14155776 | tf_op jit(solution)/shard_map/bij,bjk->bik/dot_general | solution.py:25
  159.9 11.7 %copy.10 = f32[288,64,64]{0,2,1:T(8,128)} copy(f32[288,64,64]{1,2,0:T(8,128)} %convolution_bitcast_fusion.1) | data formatting | bytes 9437184 | tf_op jit(solution)/shard_map/bij,bjk->bik/dot_general | solution.py:25
  171.6 12.3 %fusion.5 = f32[384,4096]{1,0:T(8,128)} fusion(f32[288,4096]{0,1:T(8,128)} %bitcast.31, s32[288]{0:T(512)S(1)} %get-tuple-element.9), kind=kOutput, calls=%fused_computation.15 | convolution fusion | flops 5435928576 | bytes 11011200 | tf_op jit(solution)/shard_map/dot_general | solution.py:29
  183.9 10.8 %reshape.223 = f32[24576,64]{1,0:T(8,128)} reshape(f32[384,4096]{1,0:T(8,128)} %fusion.5) | data formatting | bytes 12582912 | tf_op jit(solution)/shard_map/reshape | solution.py:35
  194.7 0.0 reduce-scatter.3.cloned.1.call-update
  194.7 0.0 all-gather.5.cloned.1.call-start
  194.8 90.7 %reduce-scatter.3.cloned.1.call-done = f32[3072,64]{1,0:T(8,128)} async-done(((f32[24576,64]{1,0:T(8,128)}), f32[3072,64]{1,0:T(8,128)}) %reduce-scatter.3.cloned.1.call-update) | async-done | bytes 786448 | tf_op jit(solution)/shard_map/reduce_scatter | solution.py:58
  285.5 0.0 copy-start.1
  285.5 1.9 multiply_reduce_fusion
  287.4 11.7 %psum.14 = f32[64]{0:T(128)S(1)} all-reduce(f32[64]{0:T(128)S(1)} %multiply_reduce_fusion), channel_id=1, replica_groups=mesh['row'=8,'col'=4] {'col'}, use_global_device_ids=true, to_apply=%region_2.3 | all-reduce | flops 64 | bytes 512 | tf_op jit(solution)/shard_map/psum | solution.py:59
  299.1 11.8 %psum.15 = f32[64]{0:T(128)S(1)} all-reduce(f32[64]{0:T(128)S(1)} %psum.14), channel_id=1, replica_groups=mesh['row'=8,'col'=4] {'row'}, use_global_device_ids=true, to_apply=%region_3.4 | all-reduce | flops 64 | bytes 512 | tf_op jit(solution)/shard_map/psum | solution.py:59
  310.9 0.0 copy-done.1
  310.9 1.3 broadcast_divide_fusion
  312.2 0.0 all-gather.5.cloned.1.call-update
  312.2 0.0 reduce-scatter.5.cloned.1.call-start
  312.3 69.3 %all-gather.5.cloned.1.call-done = f32[24576,64]{1,0:T(8,128)} async-done(((f32[3072,64]{1,0:T(8,128)}), f32[24576,64]{1,0:T(8,128)}) %all-gather.5.cloned.1.call-update) | async-done | bytes 6291472 | tf_op jit(solution)/shard_map/all_gather | solution.py:61
  381.6 9.4 %gather_fusion.1 = f32[288,64,64]{2,1,0:T(8,128)} fusion(f32[384,64,64]{2,1,0:T(8,128)} %bitcast.34, s32[1024]{0:T(1024)S(1)} %pad_clamp_fusion), kind=kCustom, calls=%fused_computation.1 | custom fusion | bytes 9438336 | tf_op jit(solution)/shard_map/gather | solution.py:23
  391.0 21.1 %convolution_bitcast_fusion = f32[288,64,64]{1,2,0:T(8,128)} fusion(f32[288,64,64]{2,1,0:T(8,128)} %gather_fusion.1, f32[288,64,64]{2,1,0:T(8,128)} %copy.9), kind=kOutput, calls=%fused_computation.2 | convolution fusion | flops 905969664 | bytes 14155776 | tf_op jit(solution)/shard_map/bji,bjk->bik/dot_general | solution.py:25
  412.1 11.6 %copy.15 = f32[288,64,64]{0,2,1:T(8,128)} copy(f32[288,64,64]{1,2,0:T(8,128)} %convolution_bitcast_fusion) | data formatting | bytes 9437184 | tf_op jit(solution)/shard_map/bji,bjk->bik/dot_general | solution.py:25
  423.7 5.9 %fusion.7 = f32[192,4096]{1,0:T(8,128)S(1)} fusion(f32[288,4096]{0,1:T(8,128)} %bitcast.30, s32[288]{0:T(512)S(1)} %get-tuple-element.8), kind=kOutput, calls=%fused_computation.18 | convolution fusion | flops 2717964288 | bytes 7865472 | tf_op jit(solution)/shard_map/dot_general | solution.py:29
  429.6 4.2 reshape.226
  433.9 0.0 copy-start
  433.9 0.0 reduce-scatter.5.cloned.1.call-update
  433.9 1.4 copy-done
  435.3 1.3 copy.16
  436.6 108.2 %reduce-scatter.5.cloned.1.call-done = f32[3072,64]{1,0:T(8,128)} async-done(((f32[12288,64]{1,0:T(8,128)}), f32[3072,64]{1,0:T(8,128)}) %reduce-scatter.5.cloned.1.call-update) | async-done | bytes 786448 | tf_op jit(solution)/shard_map/reduce_scatter | solution.py:63
  544.8 2.7 copy.17
  (15 shorter events, 0.2 us)
Async XLA Ops:
  7.2 123.7 %all-gather.3.cloned.1.call-start = ((), (), s32[]{:S(2)}) async-start(), calls=%async_computation.2 | async-start | bytes 7864320 | tf_op jit(solution)/shard_map/all_gather | solution.py:56
  12.7 272.8 %reduce-scatter.3.cloned.1.call-start = ((), (), s32[]{:S(2)}) async-start(), calls=%async_computation.3 | async-start | bytes 14155776 | tf_op jit(solution)/shard_map/reduce_scatter | solution.py:58
  19.0 12.3 %copy-start.2 = (s32[1,1,288]{2,1,0:T(1,128)S(1)}, s32[1,1,288]{2,1,0:T(1,128)}, u32[]{:S(2)}) copy-start(s32[1,1,288]{2,1,0:T(1,128)} %param.4) | copy-start | bytes 3460
  194.7 186.9 %all-gather.5.cloned.1.call-start = ((), (), s32[]{:S(2)}) async-start(), calls=%async_computation.4 | async-start | bytes 14155776 | tf_op jit(solution)/shard_map/all_gather | solution.py:61
  285.5 25.4 %copy-start.1 = (f32[3072,64]{1,0:T(8,128)S(1)}, f32[3072,64]{1,0:T(8,128)}, u32[]{:S(2)}) copy-start(f32[3072,64]{1,0:T(8,128)} %reduce-scatter.3.cloned.1.call-done) | copy-start | bytes 2359300
  312.2 232.6 %reduce-scatter.5.cloned.1.call-start = ((), (), s32[]{:S(2)}) async-start(), calls=%async_computation.5 | async-start | bytes 7864320 | tf_op jit(solution)/shard_map/reduce_scatter | solution.py:63
  433.9 1.4 copy-start
Sparse Core Ops, SparseCore 0:
  12.8 118.0 all-gather.2
  194.8 90.6 reduce-scatter.2
  312.4 69.2 all-gather.4
  434.0 110.7 reduce-scatter.4
